TPU v7x, 256 devices: a whole 4x4x8 slice. The times are simulated.
256 devices in a mesh: row: 16 (over y, x), col: 16 (over z, core).
Axes of the slice: x: 4, y: 4, z: 8, core: 2. Of those that a mesh axis runs over, the one named last changes fastest.
Arguments:
- term_matrix: bfloat16 [12288, 32768], P('row', 'col'), may hold values from -6 to 6
- sign_bits: int32 [32768], P('col'), may hold values from 0 to 1
- sampled: int32 [256, 512], P('col'), may hold values from 0 to 127
Outputs:
- projected: float32 [512, 32768], P('row', 'col')
All inputs are finite; a program needn't handle non-finite values.
Results may differ from a plain program's by a relative error of at most 0.0025.
Values may be sent and summed in bfloat16 or wider, within the bound.
A program may use at most 64 MiB of HBM per device.

v0:
```python
import jax
import jax.numpy as jnp
from jax import lax
from jax.sharding import PartitionSpec as P


def bit_parity(value):
    total = jnp.zeros_like(value)
    for bit_pos in range(7):
        total = total + (value >> bit_pos & 1)
    return total & 1


def hadamard_cols(sign_part, sample_part):
    blocks = sample_part.shape[0]
    hrange = lax.iota(jnp.int32, 128)
    parity = bit_parity(hrange[None, :, None] & sample_part[:, None, :])
    values = (1 - 2 * parity) * (2 * sign_part.reshape(blocks, 128, 1) - 1)
    return values.reshape(blocks * 128, sample_part.shape[1]).astype(jnp.bfloat16)


def sketch_block(a_rows, sign_bits, sampled):
    group_cols = min(1024, a_rows.shape[1])
    groups = a_rows.shape[1] // group_cols
    per_group = group_cols // 128

    def advance(running, group_idx):
        a_part = lax.dynamic_slice_in_dim(a_rows, group_idx * group_cols, group_cols, 1)
        sign_part = lax.dynamic_slice_in_dim(sign_bits, group_idx * group_cols, group_cols, 0)
        sample_part = lax.dynamic_slice_in_dim(sampled, group_idx * per_group, per_group, 0)
        sketch_cols = hadamard_cols(sign_part, sample_part)
        return (running + jnp.dot(a_part, sketch_cols, preferred_element_type=jnp.float32), None)

    start_sum = jnp.zeros((a_rows.shape[0], sampled.shape[1]), jnp.float32)
    running, ignored = lax.scan(advance, start_sum, jnp.arange(groups, dtype=jnp.int32))
    return running


def gram_of(sketch_part):
    return jnp.dot(
        sketch_part.T,
        sketch_part,
        precision=lax.Precision.HIGHEST,
        preferred_element_type=jnp.float32,
    )


def basis_from(factor, sketch_part):
    return jax.scipy.linalg.solve_triangular(factor, sketch_part.T, lower=True).astype(jnp.bfloat16)


def shards(term_matrix, sign_bits, sampled):
    partial_sketch = sketch_block(term_matrix, sign_bits, sampled)
    sketch = lax.psum(partial_sketch, "col")
    gram_sum = lax.psum(gram_of(sketch), "row")
    basis_t = basis_from(jnp.linalg.cholesky(gram_sum), sketch)
    return lax.psum_scatter(
        jnp.dot(basis_t, term_matrix, preferred_element_type=jnp.float32),
        "row",
        scatter_dimension=0,
        tiled=True,
    )


def solution(mesh):
    in_specs = (P("row", "col"), P("col"), P("col", None))
    out_specs = P("row", "col")
    return jax.shard_map(shards, mesh=mesh, in_specs=in_specs, out_specs=out_specs, check_vma=False)
```

profile of v0, /device:TPU:1, one launch (start us, length us, event | category | flops | bytes accessed | tf_op | source)
XLA Modules:
  0.0 486.8 jit_solution(5646887887728623750)
XLA Ops:
  6.5 16.3 %while.15 = (s32[]{:T(128)}, f32[768,512]{1,0:T(8,128)S(1)}, s32[2]{0:T(128)S(1)}, bf16[768,2048]{1,0:T(8,128)(2,1)}, s32[16,512]{1,0:T(8,128)}, /*index=5*/s32[...) while((s32[]{:T(128)}, f32[768,512]{1,0:T(8,128)S(1)}, ...), condition=%wide.region_1.2_spmd.clone, body=%wide.region_0.1_spmd.clone.sunk | while | flops 819726336 | bytes 6885619 | solution.py:35
  6.5 0.7 dynamic_slice.42
  7.9 0.7 multiply_add_fusion.2
  9.3 0.7 constant_dynamic-slice_fusion.5
  10.0 2.0 fusion.89
  12.1 2.6 select_add_fusion.2
  14.7 0.7 dynamic_slice.42
  16.0 0.7 multiply_add_fusion.2
  17.4 0.7 constant_dynamic-slice_fusion.5
  18.2 2.0 fusion.89
  20.2 2.6 select_add_fusion.2
  22.8 1.1 copy-done.3
  24.0 116.9 %all-reduce.4.cloned.1.call-done = f32[768,512]{1,0:T(8,128)} async-done(((f32[768,512]{1,0:T(8,128)}), f32[768,512]{1,0:T(8,128)}) %all-reduce.4.cloned.1.call-update) | async-done | bytes 1572880 | tf_op jit(solution)/shard_map/psum | solution.py:54
  141.0 5.6 %fusion.72 = f32[512,512]{0,1:T(8,128)} fusion(f32[768,512]{1,0:T(8,128)} %all-reduce.4.cloned.1.call-done), kind=kOutput, calls=%fused_computation.111 | convolution fusion | flops 2415919104 | bytes 2621440 | tf_op jit(solution)/shard_map/dot_general | solution.py:40
  146.8 96.0 %all-reduce.6.cloned.1.call-done = f32[512,512]{0,1:T(8,128)} async-done(((f32[512,512]{0,1:T(8,128)}), f32[512,512]{0,1:T(8,128)}) %all-reduce.6.cloned.1.call-update) | async-done | bytes 1048592 | tf_op jit(solution)/shard_map/psum | solution.py:55
  242.8 1.6 copy.5
  244.7 1.0 copy-done.2
  245.7 11.7 %cholesky.104 = f32[128,128]{1,0:T(8,128)S(1)} custom-call(f32[128,128]{1,0:T(8,128)S(1)} %cholesky.266), custom_call_target="Cholesky" | custom-call | tf_op jit(solution)/shard_map/jit(cholesky)/cholesky | solution.py:56
  257.4 9.8 %custom-call.31 = f32[1,128,128]{1,2,0:T(8,128)S(1)} custom-call(f32[1,128,128]{2,1,0:T(8,128)S(1)} %get-tuple-element.143), custom_call_target="InvertDiagBlocksLowerTriangular" | custom-call | tf_op jit(solution)/shard_map/jit(cholesky)/cholesky | solution.py:56
  267.4 1.2 constant_dynamic-update-slice_fusion.3
  268.6 1.3 convolution_subtract_fusion.3
  269.9 11.7 %cholesky.217 = f32[128,128]{1,0:T(8,128)S(1)} custom-call(f32[128,128]{1,0:T(8,128)S(1)} %cholesky.270), custom_call_target="Cholesky" | custom-call | tf_op jit(solution)/shard_map/jit(cholesky)/cholesky | solution.py:56
  281.6 10.0 %custom-call.32 = f32[1,128,128]{1,2,0:T(8,128)S(1)} custom-call(f32[1,128,128]{2,1,0:T(8,128)S(1)} %get-tuple-element.140), custom_call_target="InvertDiagBlocksLowerTriangular" | custom-call | tf_op jit(solution)/shard_map/jit(cholesky)/cholesky | solution.py:56
  291.9 1.3 convolution_subtract_fusion.4
  293.2 11.7 %cholesky.238 = f32[128,128]{1,0:T(8,128)S(1)} custom-call(f32[128,128]{1,0:T(8,128)S(1)} %cholesky.275), custom_call_target="Cholesky" | custom-call | tf_op jit(solution)/shard_map/jit(cholesky)/cholesky | solution.py:56
  305.0 0.7 compare_reduce_fusion.1
  305.6 9.8 %custom-call.33 = f32[1,128,128]{1,2,0:T(8,128)S(1)} custom-call(f32[1,128,128]{2,1,0:T(8,128)S(1)} %get-tuple-element.137), custom_call_target="InvertDiagBlocksLowerTriangular" | custom-call | tf_op jit(solution)/shard_map/jit(cholesky)/cholesky | solution.py:56
  315.6 1.2 convolution_subtract_fusion.5
  316.9 11.7 %cholesky.255 = f32[128,128]{1,0:T(8,128)S(1)} custom-call(f32[128,128]{1,0:T(8,128)S(1)} %convolution_subtract_fusion.5), custom_call_target="Cholesky" | custom-call | tf_op jit(solution)/shard_map/jit(cholesky)/cholesky | solution.py:56
  328.6 0.7 compare_reduce_fusion
  329.3 0.7 compare_reduce_fusion.2
  332.5 1.3 select_select_fusion
  333.8 11.6 %while.14 = (s32[]{:T(128)}, f32[512,512]{1,0:T(8,128)}, s32[4,2]{0,1:T(2,128)S(1)}, f32[4,128,128]{2,1,0:T(8,128)S(1)}, s32[]{:T(128)}) while((s32[]{:T(128)}, f32[512,512]{1,0:T(8,128)}, s32[4,2]{0,1:T(2,128)S(1)}, f32[4,128,128]{2,1,0:T(8,128)S(1)}, s32[]{:T(128)}) %tuple.58), condition=%wide.while_cond, body=%wide.while_body.sunk | while | flops 2 | bytes 131181 | solution.py:49
  333.9 0.6 fusion.86
  334.5 2.3 bitcast_dynamic-update-slice_fusion.2
  336.8 0.6 fusion.86
  337.4 2.3 bitcast_dynamic-update-slice_fusion.2
  339.8 0.6 fusion.86
  340.3 2.3 bitcast_dynamic-update-slice_fusion.2
  342.7 0.6 fusion.86
  343.3 2.2 bitcast_dynamic-update-slice_fusion.2
  345.5 39.3 %custom-call.34 = f32[4,128,128]{1,2,0:T(8,128)S(1)} custom-call(f32[4,128,128]{2,1,0:T(8,128)S(1)} %get-tuple-element.90), custom_call_target="InvertDiagBlocksLowerTriangular" | custom-call | tf_op jit(solution)/shard_map/jit(_solve_triangular)/triangular_solve | solution.py:49
  385.3 1.6 convolution_subtract_fusion.1
  387.0 0.5 fusion.70
  387.5 2.3 convolution_subtract_fusion.2
  390.4 3.3 convolution_subtract_fusion
  394.1 3.7 fusion.39
  397.9 81.9 %reduce-scatter.2.cloned.1.call-done = f32[32,2048]{1,0:T(8,128)} async-done(((f32[512,2048]{1,0:T(8,128)}), f32[32,2048]{1,0:T(8,128)}) %reduce-scatter.2.cloned.1.call-update) | async-done | bytes 262160 | tf_op jit(solution)/shard_map/reduce_scatter | solution.py:57
  (39 shorter events, 3.2 us)
Async XLA Ops:
  6.5 134.4 %all-reduce.4.cloned.1.call-start = ((), (), s32[]{:S(2)}) async-start(), calls=%async_computation.1 | async-start | bytes 3145728 | tf_op jit(solution)/shard_map/psum | solution.py:54
  22.8 1.1 copy-start.3
  24.0 218.8 %all-reduce.6.cloned.1.call-start = ((), (), s32[]{:S(2)}) async-start(), calls=%async_computation.2 | async-start | bytes 2097152 | tf_op jit(solution)/shard_map/psum | solution.py:55
  146.6 333.2 %reduce-scatter.2.cloned.1.call-start = ((), (), s32[]{:S(2)}) async-start(), calls=%async_computation.3 | async-start | bytes 4456448 | tf_op jit(solution)/shard_map/reduce_scatter | solution.py:57
  242.8 1.7 copy-start.1
  244.7 1.0 copy-start.2
  293.2 91.6 %copy-start = (f32[768,512]{1,0:T(8,128)S(1)}, f32[768,512]{1,0:T(8,128)}, u32[]{:S(2)}) copy-start(f32[768,512]{1,0:T(8,128)} %all-reduce.4.cloned.1.call-done) | copy-start | bytes 4718596
  389.8 4.3 copy-start.4
Sparse Core Ops, SparseCore 0:
  24.1 116.8 all-reduce.3
  146.7 96.0 all-reduce.5
  398.0 81.7 reduce-scatter.1
where the time goes:
time: 492 us; the launch traced here: 487 us
  waiting for transfers between devices  295 us (60%)
  other arithmetic  125 us (25%)
  matrix products  29.3 us (6%)
  local copies, waits for them, and re-layouts  18.2 us (4%)
  between operations  16.3 us (3%)
    psum x1, waiting for transfers between devices, shards(): sketch = lax.psum(partial_sketch, 'col')  117 us
    psum x1, waiting for transfers between devices, shards(): gram_sum = lax.psum(gram_of(sketch), 'row')  96 us
    reduce_scatter x1, waiting for transfers between devices, shards(): lax.psum_scatter(jnp.dot(basis_t, term_matrix, preferred_element_type=jnp...  81.9 us
    another operation x14, other arithmetic, shards(): basis_t = basis_from(jnp.linalg.cholesky(gram_sum), sketch)  78.6 us
    another operation x3, other arithmetic, basis_from(): jax.scipy.linalg.solve_triangular(factor, sketch_part.T, lower=True)  40.6 us
    another operation x12, local copies, waits for them, and re-layouts  11.6 us
  transfers between devices with their start and end apart: 3, of which 3 were waited for; matrix products, arithmetic and copies ran while one was open for 0% of the time, Pallas kernels for 0%

commit v1 on v0

v1 whole, which is shorter than its diff:
```python
import jax
import jax.numpy as jnp
from jax import lax
from jax.experimental import pallas as pl
from jax.experimental.pallas import tpu as pltpu
from jax.sharding import PartitionSpec as P

MESH = pl.DeviceIdType.MESH
HI = lax.Precision.HIGHEST
F32 = jnp.float32
BF16 = jnp.bfloat16
STRIPS = 4
LN2 = 0.6931471805599453


def barrier(targets):
    sem = pltpu.get_barrier_semaphore()
    for target in targets:
        pl.semaphore_signal(sem, inc=1, device_id=target, device_id_type=MESH)
    return lambda: pl.semaphore_wait(sem, len(targets))


def send(src, dst, send_sem, recv_sem, target):
    copy = pltpu.make_async_remote_copy(
        src_ref=src, dst_ref=dst, send_sem=send_sem, recv_sem=recv_sem, device_id=target, device_id_type=MESH
    )
    copy.start()
    return copy


def pack(value):
    top = jnp.max(jnp.max(jnp.abs(value), axis=0, keepdims=True), axis=1, keepdims=True)
    power = jnp.ceil(jnp.log(jnp.maximum(top, 1e-30)) * (1.0 / LN2)) - 14.0
    coded = jnp.floor(value * jnp.exp(power * -LN2) + 0.5).astype(jnp.int32).astype(jnp.int16)
    return coded, jnp.broadcast_to(power, (16, 128)).astype(jnp.int32).astype(jnp.int16)


def step_of(power):
    return jnp.exp(power.astype(jnp.int32).astype(F32) * LN2)[0:1, :]


def sketch_kernel(
    a_ref, sign_ref, samp_ref, y_ref, om, mate_out, mate_in, own, part_out, part_in, full, s_mate, r_mate, s_part, r_part, s_full, r_full, s_fwd, r_fwd
):
    row, col = lax.axis_index("row"), lax.axis_index("col")
    z, core = col // 2, lax.rem(col, 2)
    mate = (row, 2 * z + 1 - core)

    def chip(distance):
        return (row, 2 * lax.rem(z + distance, 8) + core)

    ready = barrier([mate] + [chip(d) for d in range(1, 8)])

    def make_block(block, carry):
        term = lax.broadcasted_iota(jnp.int32, (128, 512), 0)
        parity = lax.population_count(term & samp_ref[block]) & 1
        om[pl.ds(pl.multiple_of(block * 128, 128), 128), :] = (1 - 2 * parity).astype(F32).astype(BF16)
        return carry

    lax.fori_loop(0, 16, make_block, 0)
    signs = (2 * sign_ref[...] - 1).astype(F32).astype(BF16)

    def half(which, out):
        rows = a_ref[pl.ds(pl.multiple_of(which * 384, 384), 384), :] * signs
        for n in range(2):
            out(n, jnp.dot(rows, om[:, 256 * n : 256 * n + 256], preferred_element_type=F32))

    mate_copies = []

    def to_mate(n, value):
        mate_out[n] = value
        if n == 0:
            ready()
        mate_copies.append(send(mate_out.at[n], mate_in.at[n], s_mate.at[n], r_mate.at[n], mate))

    def keep(n, value):
        own[:, 256 * n : 256 * n + 256] = value

    half(1 - core, to_mate)
    half(core, keep)
    for n in range(2):
        mate_copies[n].wait_recv()
        own[:, 256 * n : 256 * n + 256] += mate_in[n]

    part_copies = []
    for d in (4, 3, 5, 2, 6, 1, 7):
        there = lax.rem(z + d, 8)
        coded, power = pack(own[pl.ds(pl.multiple_of(there * 48, 48), 48), :])
        for j in range(4):
            part_out[d, 48 * j : 48 * j + 48, :] = coded[:, 128 * j : 128 * j + 128]
        part_out[d, 192:208, :] = power
        part_copies.append(send(part_out.at[d], part_in.at[d], s_part.at[d], r_part.at[d], chip(d)))
    for copy in part_copies:
        copy.wait_recv()
    slot = core * 8 + z
    scales = [step_of(part_in[d, 192:208, :]) for d in range(1, 8)]
    for j in range(4):
        total = own[pl.ds(pl.multiple_of(z * 48, 48), 48), 128 * j : 128 * j + 128]
        for d in range(1, 8):
            total = total + part_in[d, 48 * j : 48 * j + 48, :].astype(jnp.int32).astype(F32) * scales[d - 1]
        full[slot, :, 128 * j : 128 * j + 128] = total.astype(BF16)

    full_copies = []
    for d in (4, 3, 5, 2, 6, 1, 7):
        full_copies.append((d, send(full.at[slot], full.at[slot], s_full.at[d], r_full.at[d], chip(d))))
    fwd_copies = [send(full.at[slot], full.at[slot], s_fwd.at[0], r_fwd.at[0], mate)]
    for d, copy in reversed(full_copies):
        copy.wait_recv()
        came = core * 8 + lax.rem(z + 8 - d, 8)
        fwd_copies.append(send(full.at[came], full.at[came], s_fwd.at[d], r_fwd.at[d], mate))
    for copy in fwd_copies:
        copy.wait_recv()
    for s in range(16):
        y_ref[48 * s : 48 * s + 48, :] = full[s]
    for copy in mate_copies + part_copies + [c for _, c in full_copies] + fwd_copies:
        copy.wait_send()


def sketch(term_matrix, sign_bits, sampled):
    vmem = pl.BlockSpec(memory_space=pltpu.VMEM)
    return pl.pallas_call(
        sketch_kernel,
        out_shape=jax.ShapeDtypeStruct((768, 512), BF16),
        in_specs=[vmem, vmem, vmem],
        out_specs=vmem,
        scratch_shapes=[
            pltpu.VMEM((2048, 512), BF16),
            pltpu.VMEM((2, 384, 256), F32),
            pltpu.VMEM((2, 384, 256), F32),
            pltpu.VMEM((384, 512), F32),
            pltpu.VMEM((8, 208, 128), jnp.int16),
            pltpu.VMEM((8, 208, 128), jnp.int16),
            pltpu.VMEM((16, 48, 512), BF16),
            pltpu.SemaphoreType.DMA((2,)),
            pltpu.SemaphoreType.DMA((2,)),
            pltpu.SemaphoreType.DMA((8,)),
            pltpu.SemaphoreType.DMA((8,)),
            pltpu.SemaphoreType.DMA((8,)),
            pltpu.SemaphoreType.DMA((8,)),
            pltpu.SemaphoreType.DMA((8,)),
            pltpu.SemaphoreType.DMA((8,)),
        ],
        compiler_params=pltpu.CompilerParams(collective_id=0, has_side_effects=True, vmem_limit_bytes=48 << 20),
    )(term_matrix, sign_bits.reshape(1, 2048), sampled.reshape(16, 1, 512))


def lane_of(x, lane):
    return jnp.broadcast_to(x[:, lane : lane + 1], (8, 128))


def dot_t(a, b):
    return lax.dot_general(a, b, (((0,), (0,)), ((), ())), precision=HI, preferred_element_type=F32)


def dot_hi(a, b):
    return jnp.dot(a, b, precision=HI, preferred_element_type=F32)


def factor_block(x, w, base):
    for t in range(16):
        at = 8 * t
        strip = x[t, :, 0:128]
        for j in range(8):
            x[20 + j // 2, :, 128 * (j % 2) : 128 * (j % 2) + 128] = lane_of(strip, at + j)
        left = [jnp.broadcast_to(x[t, i : i + 1, 0:128], (8, 128)) for i in range(8)]
        right = [jnp.broadcast_to(x[t, i : i + 1, 128:256], (8, 128)) for i in range(8)]
        a = [[None] * 8 for _ in range(8)]
        for i in range(8):
            for j in range(i, 8):
                a[i][j] = jnp.broadcast_to(x[20 + j // 2, i : i + 1, 128 * (j % 2) : 128 * (j % 2) + 128], (8, 128))
        recips, mult = [], [[None] * 8 for _ in range(8)]
        for k in range(8):
            recips.append(1.0 / a[k][k])
            for j in range(k + 1, 8):
                mult[k][j] = a[k][j] * recips[k]
            for i in range(k + 1, 8):
                for j in range(i, 8):
                    a[i][j] = a[i][j] - mult[k][i] * a[k][j]
            for j in range(k + 1, 8):
                left[j] = left[j] - mult[k][j] * left[k]
                right[j] = right[j] - mult[k][j] * right[k]
        last = STRIPS * (t // STRIPS) + STRIPS
        for k in range(8):
            scale = lax.rsqrt(a[k][k])
            w[base // 8 + t, k : k + 1, :] = (right[k] * scale)[0:1]
            if last < 16:
                x[16 + t % STRIPS, k : k + 1, 0:128] = (left[k] * scale)[0:1]
                x[16 + t % STRIPS, k : k + 1, 128:256] = (right[k] * scale)[0:1]
        if t + 1 < last:
            v_left, v_right = [None] * 8, [None] * 8
            for i in range(7, -1, -1):
                vl, vr = left[i] * recips[i], right[i] * recips[i]
                for j in range(7, i, -1):
                    vl = vl - mult[i][j] * v_left[j]
                    vr = vr - mult[i][j] * v_right[j]
                v_left[i], v_right[i] = vl, vr
            for s in range(t + 1, last):
                old = x[s, :, 0:128]
                new_left, new_right = old, x[s, :, 128:256]
                for k in range(8):
                    c = lane_of(old, at + k)
                    new_left = new_left - c * v_left[k]
                    new_right = new_right - c * v_right[k]
                x[s, :, 0:128] = new_left
                x[s, :, 128:256] = new_right
        elif last < 16:
            u = x[16 : 16 + STRIPS].reshape(8 * STRIPS, 256)
            change = dot_t(u[:, 0:128], u)
            x[last:16] = x[last:16] - change[8 * last :].reshape(16 - last, 8, 256)


def factor(g, x, w):
    eye = (lax.broadcasted_iota(jnp.int32, (128, 128), 0) == lax.broadcasted_iota(jnp.int32, (128, 128), 1)).astype(F32)

    def step(k, carry):
        x[0:16, :, 0:128] = g[5 * k].reshape(16, 8, 128)
        x[0:16, :, 128:256] = eye.reshape(16, 8, 128)
        factor_block(x, w, 128 * k)
        inverse = w[pl.ds(16 * k, 16)].reshape(128, 128)

        def panel(j, c):
            g[4 * k + j] = dot_hi(inverse, g[4 * k + j])
            return c

        lax.fori_loop(k + 1, 4, panel, 0)

        def outer(i, c):
            left = g[4 * k + i]

            def inner(j, cc):
                g[4 * i + j] = g[4 * i + j] - dot_t(left, g[4 * k + j])
                return cc

            return lax.fori_loop(i, 4, inner, c)

        lax.fori_loop(k + 1, 4, outer, 0)
        return carry

    lax.fori_loop(0, 4, step, 0)


TRI = [(i, j) for i in range(4) for j in range(i, 4)]


def project_kernel(
    a_ref, y_ref, o_ref, yt, gloc, gin, gfull, gsq, x, w, zf, zout, zin, pbuf, obuf,
    s_c, r_c, s_d, r_d, s_e, r_e, s_z, r_z, s_o, r_o,
):
    row, col = lax.axis_index("row"), lax.axis_index("col")
    core = lax.rem(col, 2)
    mate = (row, col + 1 - 2 * core)

    def peer(d):
        return lax.rem(row + d, 16)

    def piece(r):
        return pl.ds(pl.multiple_of(40 * (2 * r + core), 8), 40)

    ready = barrier([mate] + [(peer(d), col) for d in range(1, 16)])
    for i in range(4):
        yt[128 * i : 128 * i + 128, :] = y_ref[:, 128 * i : 128 * i + 128].T
    at = 0
    for i in range(4):
        blocks = jnp.dot(yt[128 * i : 128 * i + 128, :], y_ref[:, 128 * i :], preferred_element_type=F32)
        for j in range(4 - i):
            gloc[at : at + 128, :] = blocks[:, 128 * j : 128 * j + 128]
            at += 128
    ready()
    c_copies = []
    for d in range(1, 16):
        c_copies.append(send(gloc.at[piece(peer(d))], gin.at[d], s_c.at[d], r_c.at[d], (peer(d), col)))

    def product(n, carry):
        cols = pl.ds(pl.multiple_of(256 * n, 256), 256)
        zf[:, cols] = jnp.dot(yt[...], a_ref[:, cols], preferred_element_type=F32)
        return carry

    lax.fori_loop(0, 8, product, 0)

    def code(d, carry):
        cols = pl.ds(pl.multiple_of(128 * peer(d), 128), 128)
        coded, power = pack(zf[:, cols])
        zout[d, 0:512, :] = coded
        zout[d, 512:528, :] = power
        return carry

    lax.fori_loop(1, 16, code, 0)

    for copy in c_copies:
        copy.wait_recv()
    total = gloc[piece(row), :]
    for d in range(1, 16):
        total = total + gin[d]
    gfull[piece(row), :] = total
    d_copies, e_copies, z_copies = [], [], []
    for d in range(1, 16):
        d_copies.append(send(gfull.at[piece(row)], gfull.at[piece(row)], s_d.at[d], r_d.at[d], (peer(d), col)))
    e_copies.append(send(gfull.at[piece(row)], gfull.at[piece(row)], s_e.at[0], r_e.at[0], mate))
    for d in range(1, 16):
        z_copies.append(send(zout.at[d], zin.at[d], s_z.at[d], r_z.at[d], (peer(d), col)))
    for d in range(1, 16):
        d_copies[d - 1].wait_recv()
        came = lax.rem(row + 16 - d, 16)
        e_copies.append(send(gfull.at[piece(came)], gfull.at[piece(came)], s_e.at[d], r_e.at[d], mate))
    for copy in e_copies:
        copy.wait_recv()
    for n, (i, j) in enumerate(TRI):
        gsq[4 * i + j] = gfull[128 * n : 128 * n + 128, :]

    factor(gsq, x, w)

    for copy in z_copies:
        copy.wait_recv()

    def solve(k, carry):
        rows = pl.ds(pl.multiple_of(128 * k, 128), 128)
        value = zf[rows, pl.ds(pl.multiple_of(128 * row, 128), 128)]

        def add(d, v):
            return v + zin[d, rows, :].astype(jnp.int32).astype(F32) * step_of(zin[d, 512:528, :])

        value = lax.fori_loop(1, 16, add, value)

        def less(j, v):
            return v - dot_t(gsq[4 * j + k], pbuf[pl.ds(pl.multiple_of(128 * j, 128), 128), :])

        value = lax.fori_loop(0, k, less, value)
        pbuf[rows, :] = dot_hi(w[pl.ds(16 * k, 16)].reshape(128, 128), value)
        return carry

    lax.fori_loop(0, 4, solve, 0)

    o_copies = []
    for d in range(1, 16):
        part = pl.ds(pl.multiple_of(32 * peer(d), 32), 32)
        o_copies.append(send(pbuf.at[part], obuf.at[row], s_o.at[d], r_o.at[d], (peer(d), col)))
    obuf[row] = pbuf[pl.ds(pl.multiple_of(32 * row, 32), 32), :]
    for copy in o_copies:
        copy.wait_recv()
    for r in range(16):
        o_ref[:, 128 * r : 128 * r + 128] = obuf[r]
    for copy in c_copies + d_copies + e_copies + z_copies + o_copies:
        copy.wait_send()


def project(term_matrix, basis):
    vmem = pl.BlockSpec(memory_space=pltpu.VMEM)
    return pl.pallas_call(
        project_kernel,
        out_shape=jax.ShapeDtypeStruct((32, 2048), F32),
        in_specs=[vmem, vmem],
        out_specs=vmem,
        scratch_shapes=[
            pltpu.VMEM((512, 768), BF16),
            pltpu.VMEM((1280, 128), F32),
            pltpu.VMEM((16, 40, 128), F32),
            pltpu.VMEM((1280, 128), F32),
            pltpu.VMEM((16, 128, 128), F32),
            pltpu.VMEM((24, 8, 256), F32),
            pltpu.VMEM((64, 8, 128), F32),
            pltpu.VMEM((512, 2048), F32),
            pltpu.VMEM((16, 528, 128), jnp.int16),
            pltpu.VMEM((16, 528, 128), jnp.int16),
            pltpu.VMEM((512, 128), F32),
            pltpu.VMEM((16, 32, 128), F32),
        ]
        + [pltpu.SemaphoreType.DMA((16,))] * 10,
        compiler_params=pltpu.CompilerParams(collective_id=1, has_side_effects=True, vmem_limit_bytes=48 << 20),
    )(term_matrix, basis)


def shards(term_matrix, sign_bits, sampled):
    return project(term_matrix, sketch(term_matrix, sign_bits, sampled))


def solution(mesh):
    in_specs = (P("row", "col"), P("col"), P("col", None))
    return jax.shard_map(shards, mesh=mesh, in_specs=in_specs, out_specs=P("row", "col"), check_vma=False)
```

time: 492 us -> 105 us (0.21); the launches traced: 487 us -> 105 us
  waiting for transfers between devices: 295 us -> 0 us
  other arithmetic: 125 us -> 0 us
  Pallas kernels: 0 us -> 101 us
  matrix products: 29.3 us -> 0 us
  between operations: 16.3 us -> 0.03 us
  local copies, waits for them, and re-layouts: 18.2 us -> 4.07 us
    psum x2 -> x0, waiting for transfers between devices: 213 us -> none  [the longest x1 117 us: shards(): sketch = lax.psum(partial_sketch, 'col')]
    another operation x17 -> x0, other arithmetic: 119 us -> none  [the longest x14 78.6 us: shards(): basis_t = basis_from(jnp.linalg.cholesky(gram_sum), sketch)]
    pallas_call x0 -> x2, Pallas kernels: none -> 101 us  [the longest x1 65.1 us: project(): pl.pallas_call(project_kernel, out_shape=jax.ShapeDtypeStruct((32, 2048),...]
    reduce_scatter x1 -> x0, waiting for transfers between devices: 81.9 us -> none  [shards(): lax.psum_scatter(jnp.dot(basis_t, term_matrix, preferred_element_type=jnp...]
    another operation x13 -> x0, matrix products: 14.7 us -> none  [the longest x7 9.29 us: basis_from(): jax.scipy.linalg.solve_triangular(factor, sketch_part.T, lower=True)]
    dot_general x4 -> x0, matrix products: 14.5 us -> none  [the longest x1 5.6 us: gram_of(): jnp.dot(sketch_part.T, sketch_part, precision=lax.Precision.HIGHEST, pref...]
    another operation x17 -> x0, local copies, waits for them, and re-layouts: 11.7 us -> none
  transfers between devices with their start and end apart: 3 -> 0, of which waited for: 3 -> 0; matrix products, arithmetic and copies ran while one was open for 0% -> 0% of each run, Pallas kernels for 0% -> 0%
where the time goes in v1:
time: 105 us
  Pallas kernels  101 us (96%)
  local copies, waits for them, and re-layouts  4.07 us (4%)
    pallas_call x1, Pallas kernels, project(): pl.pallas_call(project_kernel, out_shape=jax.ShapeDtypeStruct((32, 2048),...  65.1 us
    pallas_call x1, Pallas kernels, sketch(): pl.pallas_call(sketch_kernel, out_shape=jax.ShapeDtypeStruct((768, 512),...  35.7 us
    unnamed x5, local copies, waits for them, and re-layouts  3.29 us

profile of v1, /device:TPU:1, one launch (start us, length us, event | category | flops | bytes accessed | tf_op | source)
XLA Modules:
  0.0 104.8 jit_solution(3818949099942417191)
XLA Ops:
  0.0 0.8 reshape.7.samp_ref
  0.8 0.0 copy-start
  0.8 1.9 %copy-done = bf16[768,2048]{1,0:T(8,128)(2,1)S(1)} copy-done((bf16[768,2048]{1,0:T(8,128)(2,1)S(1)}, bf16[768,2048]{1,0:T(8,128)(2,1)}, u32[]{:S(2)}) %copy-start) | copy-done | bytes 3145752
  2.7 0.0 copy-start.1
  2.7 0.7 copy-done.1
  3.4 35.7 %shard_map.37.y_ref = bf16[768,512]{1,0:T(8,128)(2,1)S(1)} custom-call(bf16[768,2048]{1,0:T(8,128)(2,1)S(1)} %copy-done, s32[1,2048]{1,0:T(1,128)S(1)} %bitcast.1, s32[16,1,512]{2,1,0:T(1,128)S(1)} %reshape.7.samp_ref), custom_call_target="tpu_custom_call" | custom-call | tf_op jit(solution)/shard_map/pallas_call | solution.py:121
  39.0 65.1 %shard_map.38 = f32[32,2048]{1,0:T(8,128)S(1)} custom-call(bf16[768,2048]{1,0:T(8,128)(2,1)S(1)} %copy-done, bf16[768,512]{1,0:T(8,128)(2,1)S(1)} %shard_map.37.y_ref), custom_call_target="tpu_custom_call" | custom-call | tf_op jit(solution)/shard_map/pallas_call | solution.py:348
  104.1 0.7 copy.5
Async XLA Ops:
  0.8 1.9 %copy-start = (bf16[768,2048]{1,0:T(8,128)(2,1)S(1)}, bf16[768,2048]{1,0:T(8,128)(2,1)}, u32[]{:S(2)}) copy-start(bf16[768,2048]{1,0:T(8,128)(2,1)} %a_ref.3) | copy-start | bytes 9437188
  2.7 0.7 copy-start.1

commit v2 on v0

v2 whole, which is shorter than its diff:
```python
import jax
import jax.numpy as jnp
from jax import lax
from jax.experimental import pallas as pl
from jax.experimental.pallas import tpu as pltpu
from jax.sharding import PartitionSpec as P

MESH = pl.DeviceIdType.MESH
F32 = jnp.float32
BF16 = jnp.bfloat16
STRIPS = 4
LN2 = 0.6931471805599453


def barrier(targets):
    sem = pltpu.get_barrier_semaphore()
    for target in targets:
        pl.semaphore_signal(sem, inc=1, device_id=target, device_id_type=MESH)
    return lambda: pl.semaphore_wait(sem, len(targets))


def send(src, dst, send_sem, recv_sem, target):
    copy = pltpu.make_async_remote_copy(
        src_ref=src, dst_ref=dst, send_sem=send_sem, recv_sem=recv_sem, device_id=target, device_id_type=MESH
    )
    copy.start()
    return copy


def pack(value):
    top = jnp.max(jnp.max(jnp.abs(value), axis=0, keepdims=True), axis=1, keepdims=True)
    power = jnp.ceil(jnp.log(jnp.maximum(top, 1e-30)) * (1.0 / LN2)) - 14.0
    coded = jnp.floor(value * jnp.exp(power * -LN2) + 0.5).astype(jnp.int32).astype(jnp.int16)
    return coded, jnp.broadcast_to(power, (16, 128)).astype(jnp.int32).astype(jnp.int16)


def step_of(power):
    return jnp.exp(power.astype(jnp.int32).astype(F32) * LN2)[0:1, :]


def lane_of(x, lane):
    return jnp.broadcast_to(x[:, lane : lane + 1], (8, 128))


def split(u):
    high = u.astype(BF16)
    rest = u - high.astype(F32)
    mid = rest.astype(BF16)
    return high, mid, (rest - mid.astype(F32)).astype(BF16)


def dot_t(a, b):
    ah, am, al = split(a)
    bh, bm, bl = split(b)
    left = jnp.concatenate([ah, ah, am, ah, am, al], 0)
    right = jnp.concatenate([bh, bm, bh, bl, bm, bh], 0)
    return lax.dot_general(left, right, (((0,), (0,)), ((), ())), preferred_element_type=F32)


def dot_hi(a, b):
    ah, am, al = split(a)
    bh, bm, bl = split(b)
    left = jnp.concatenate([ah, ah, am, ah, am, al], 1)
    right = jnp.concatenate([bh, bm, bh, bl, bm, bh], 0)
    return jnp.dot(left, right, preferred_element_type=F32)


def factor_block(x, w, base):
    lanes = lax.broadcasted_iota(jnp.int32, (8, 128), 1)
    for t in range(16):
        at = 8 * t
        strip = x[t]
        for j in range(8):
            x[24 + j] = lane_of(strip, at + j)
        here = (lanes >= at) & (lanes < at + 8)
        a = [[None] * 8 for _ in range(8)]
        for i in range(8):
            for j in range(i, 8):
                a[i][j] = jnp.broadcast_to(x[24 + j, i : i + 1, :], (8, 128))
        rows = [jnp.where(here, (lanes == at + i).astype(F32), jnp.broadcast_to(x[t, i : i + 1, :], (8, 128))) for i in range(8)]
        recips, mult = [], [[None] * 8 for _ in range(8)]
        for k in range(8):
            recips.append(1.0 / a[k][k])
            for j in range(k + 1, 8):
                mult[k][j] = a[k][j] * recips[k]
            for i in range(k + 1, 8):
                for j in range(i, 8):
                    a[i][j] = a[i][j] - mult[k][i] * a[k][j]
            for j in range(k + 1, 8):
                rows[j] = rows[j] - mult[k][j] * rows[k]
        last = STRIPS * (t // STRIPS) + STRIPS
        done = lanes < at + 8
        for k in range(8):
            u = rows[k] * lax.rsqrt(a[k][k])
            w[base // 8 + t, k : k + 1, :] = jnp.where(done, u, 0.0)[0:1]
            if last < 16:
                x[16 + t % STRIPS, k : k + 1, :] = jnp.where(done | (lanes >= 8 * last), u, 0.0)[0:1]
        if t + 1 < last:
            v = [None] * 8
            for i in range(7, -1, -1):
                v[i] = rows[i] * recips[i]
                for j in range(7, i, -1):
                    v[i] = v[i] - mult[i][j] * v[j]
            for s in range(t + 1, last):
                old = x[s]
                new = jnp.where(here, 0.0, old)
                for k in range(8):
                    new = new - lane_of(old, at + k) * v[k]
                x[s] = new
        elif last < 16:
            u = x[16 : 16 + STRIPS].reshape(8 * STRIPS, 128)
            change = dot_t(u, u)[8 * last :].reshape(16 - last, 8, 128)
            inside = (lanes >= 8 * (last - STRIPS)) & (lanes < 8 * last)
            x[last:16] = jnp.where(inside[None], 0.0, x[last:16]) - change


def factor(g, x, w, between):
    def step(k, carry):
        between(k)
        x[0:16] = g[5 * k].reshape(16, 8, 128)
        factor_block(x, w, 128 * k)
        inverse = w[pl.ds(16 * k, 16)].reshape(128, 128)

        def panel(j, c):
            g[4 * k + j] = dot_hi(inverse, g[4 * k + j])
            return c

        lax.fori_loop(k + 1, 4, panel, 0)

        def outer(i, c):
            left = g[4 * k + i]

            def inner(j, cc):
                g[4 * i + j] = g[4 * i + j] - dot_t(left, g[4 * k + j])
                return cc

            return lax.fori_loop(i, 4, inner, c)

        lax.fori_loop(k + 1, 4, outer, 0)
        return carry

    lax.fori_loop(0, 4, step, 0)


TRI = [(i, j) for i in range(4) for j in range(i, 4)]
FAR_FIRST = (4, 3, 5, 2, 6, 1, 7)
NEAR_FIRST = FAR_FIRST[::-1]
MID = 2


def kernel(
    a_hbm, sign_ref, samp_ref, o_ref,
    a, om, mate_out, mate_in, own, part_out, part_in, full, yt, gloc, gin, gfull, gsq, x, w,
    zf, zs1, zr1, zs2, zr2, zown, pbuf, obuf,
    s_a, s_mate, r_mate, s_part, r_part, s_full, r_full, s_fwd, r_fwd,
    s_c, r_c, s_d, r_d, s_e, r_e, s_z1, r_z1, s_z2, r_z2, s_o, r_o,
):
    row, col = lax.axis_index("row"), lax.axis_index("col")
    z, core = col // 2, lax.rem(col, 2)
    py, px = row // 4, lax.rem(row, 4)
    mate = (row, 2 * z + 1 - core)

    def chip(distance):
        return (row, 2 * lax.rem(z + distance, 8) + core)

    def peer(d):
        return lax.rem(row + d, 16)

    def half_rows(which):
        return pl.ds(pl.multiple_of(which * 384, 384), 384)

    loads = []
    for n, which in enumerate((1 - core, core)):
        loads.append(pltpu.make_async_copy(a_hbm.at[half_rows(which)], a.at[half_rows(which)], s_a.at[n]))
        loads[n].start()
    ready = barrier([mate] + [chip(d) for d in range(1, 8)] + [(peer(d), col) for d in range(1, 16)])

    term = lax.broadcasted_iota(jnp.int32, (128, 512), 0)
    for block in range(16):
        parity = lax.population_count(term & samp_ref[block : block + 1, :]) & 1
        om[128 * block : 128 * block + 128, :] = (1 - 2 * parity).astype(F32).astype(BF16)
    signs = (2 * sign_ref[...] - 1).astype(F32).astype(BF16)

    def partial(which, n):
        rows = a[half_rows(which), :] * signs
        return jnp.dot(rows, om[:, 256 * n : 256 * n + 256], preferred_element_type=F32)

    mate_copies, part_copies, full_copies, fwd_copies = [], [], [], []
    loads[0].wait()
    for n in range(2):
        mate_out[n] = partial(1 - core, n)
        if n == 0:
            ready()
        mate_copies.append(send(mate_out.at[n], mate_in.at[n], s_mate.at[n], r_mate.at[n], mate))
    loads[1].wait()
    for n in range(2):
        own[n] = partial(core, n)
        mate_copies[n].wait_recv()
        own[n] += mate_in[n]
        for d in FAR_FIRST:
            there = lax.rem(z + d, 8)
            coded, power = pack(own[n, pl.ds(pl.multiple_of(there * 48, 48), 48), :])
            part_out[n, d, 0:48, :] = coded[:, 0:128]
            part_out[n, d, 48:96, :] = coded[:, 128:256]
            part_out[n, d, 96:112, :] = power
            part_copies.append(send(part_out.at[n, d], part_in.at[n, d], s_part.at[n, d], r_part.at[n, d], chip(d)))
    slot = core * 8 + z
    for n in range(2):
        for copy in part_copies[7 * n : 7 * n + 7]:
            copy.wait_recv()
        for j in range(2):
            total = own[n, pl.ds(pl.multiple_of(z * 48, 48), 48), 128 * j : 128 * j + 128]
            for d in range(1, 8):
                value = part_in[n, d, 48 * j : 48 * j + 48, :].astype(jnp.int32).astype(F32)
                total = total + value * step_of(part_in[n, d, 96:112, :])
            full[n, slot, :, 128 * j : 128 * j + 128] = total.astype(BF16)
        mine = full.at[n, slot]
        for d in FAR_FIRST:
            full_copies.append(send(mine, mine, s_full.at[n, d], r_full.at[n, d], chip(d)))
        fwd_copies.append(send(mine, mine, s_fwd.at[n, 0], r_fwd.at[n, 0], mate))
    for n in range(2):
        for m, d in enumerate(FAR_FIRST):
            full_copies[7 * n + m].wait_recv()
            came = full.at[n, core * 8 + lax.rem(z + 8 - d, 8)]
            fwd_copies.append(send(came, came, s_fwd.at[n, d], r_fwd.at[n, d], mate))
    for copy in fwd_copies:
        copy.wait_recv()

    def piece(r):
        return pl.ds(pl.multiple_of(40 * (2 * r + core), 8), 40)

    for i in range(4):
        yt[128 * i : 128 * i + 128, :] = full[i // 2, :, :, 128 * (i % 2) : 128 * (i % 2) + 128].reshape(768, 128).T
    for i in range(4):
        for n in range(i // 2, 2):
            blocks = jnp.dot(yt[128 * i : 128 * i + 128, :], full[n].reshape(768, 256), preferred_element_type=F32)
            for j in range(2 * n, 2 * n + 2):
                if j >= i:
                    at = 128 * TRI.index((i, j))
                    gloc[at : at + 128, :] = blocks[:, 128 * (j - 2 * n) : 128 * (j - 2 * n) + 128]
    c_copies, d_copies, e_copies, o_copies = [], [], [], []
    for d in range(1, 16):
        c_copies.append(send(gloc.at[piece(peer(d))], gin.at[d], s_c.at[d], r_c.at[d], (peer(d), col)))

    def product(n, carry):
        cols = pl.ds(pl.multiple_of(256 * n, 256), 256)
        zf[:, cols] = jnp.dot(yt[...], a[:, cols], preferred_element_type=F32)
        return carry

    lax.fori_loop(0, 8, product, 0)

    def along(h, d, e):
        return (4 * e + lax.rem(px + d, 4)) if h == 0 else (4 * lax.rem(py + d, 4) + e)

    def first(h, d):
        target = (along(h, d, py if h == 0 else px), col)
        return pltpu.make_async_remote_copy(
            src_ref=zs1.at[h, d], dst_ref=zr1.at[h, d], send_sem=s_z1.at[h, d], recv_sem=r_z1.at[h, d], device_id=target, device_id_type=MESH
        )

    def second(h, d):
        target = (along(1 - h, d, px if h == 0 else py), col)
        return pltpu.make_async_remote_copy(
            src_ref=zs2.at[h, d], dst_ref=zr2.at[h, d], send_sem=s_z2.at[h, d], recv_sem=r_z2.at[h, d], device_id=target, device_id_type=MESH
        )

    def z_part(h, r):
        return zf[256 * h : 256 * h + 256, pl.ds(pl.multiple_of(128 * r, 128), 128)]

    for h in range(2):

        def code(m, carry):
            d, e = m // 4 + 1, lax.rem(m, 4)
            coded, power = pack(z_part(h, along(h, d, e)))
            zs1[h, d, e, 0:256, :] = coded
            zs1[h, d, e, 256:272, :] = power
            return carry

        lax.fori_loop(0, 12, code, 0)

    for copy in c_copies:
        copy.wait_recv()
    total = gloc[piece(row), :]
    for d in range(1, 16):
        total = total + gin[d]
    gfull[piece(row), :] = total
    mine = gfull.at[piece(row)]
    for d in range(1, 16):
        d_copies.append(send(mine, mine, s_d.at[d], r_d.at[d], (peer(d), col)))
    e_copies.append(send(mine, mine, s_e.at[0], r_e.at[0], mate))
    for d in (2, 1, 3):
        for h in range(2):
            first(h, d).start()
    for d in range(1, 16):
        d_copies[d - 1].wait_recv()
        came = gfull.at[piece(lax.rem(row + 16 - d, 16))]
        e_copies.append(send(came, came, s_e.at[d], r_e.at[d], mate))
    for copy in e_copies:
        copy.wait_recv()
    for n, (i, j) in enumerate(TRI):
        gsq[4 * i + j] = gfull[128 * n : 128 * n + 128, :]

    def between(k):
        @pl.when(k == MID)
        def _():
            for h in range(2):
                for d in range(1, 4):
                    first(h, d).wait_recv()

                def add(d, carry):
                    e = lax.rem((py if h == 0 else px) + d, 4)
                    value = z_part(h, along(h, 0, e))
                    for f in range(1, 4):
                        step = step_of(zr1[h, f, e, 256:272, :])
                        value = value + zr1[h, f, e, 0:256, :].astype(jnp.int32).astype(F32) * step
                    zown[h, d] = value
                    coded, power = pack(value)
                    zs2[h, d, 0:256, :] = coded
                    zs2[h, d, 256:272, :] = power
                    return carry

                lax.fori_loop(0, 4, add, 0)
                for d in range(1, 4):
                    second(h, d).start()

    factor(gsq, x, w, between)

    for h in range(2):
        for d in range(1, 4):
            second(h, d).wait_recv()
        value = zown[h, 0]
        for d in range(1, 4):
            step = step_of(zr2[h, d, 256:272, :])
            value = value + zr2[h, d, 0:256, :].astype(jnp.int32).astype(F32) * step
        pbuf[256 * h : 256 * h + 256, :] = value
    for k in range(4):
        solved = dot_hi(w[16 * k : 16 * k + 16].reshape(128, 128), pbuf[128 * k : 128 * k + 128, :])
        pbuf[128 * k : 128 * k + 128, :] = solved
        for j in range(k + 1, 4):
            pbuf[128 * j : 128 * j + 128, :] -= dot_t(gsq[4 * k + j], solved)

    for d in range(1, 16):
        part = pl.ds(pl.multiple_of(32 * peer(d), 32), 32)
        o_copies.append(send(pbuf.at[part], obuf.at[row], s_o.at[d], r_o.at[d], (peer(d), col)))
    obuf[row] = pbuf[pl.ds(pl.multiple_of(32 * row, 32), 32), :]
    for copy in o_copies:
        copy.wait_recv()
    for r in range(16):
        o_ref[:, 128 * r : 128 * r + 128] = obuf[r]
    for copy in mate_copies + part_copies + full_copies + fwd_copies + c_copies + d_copies + e_copies + o_copies:
        copy.wait_send()
    for h in range(2):
        for d in range(1, 4):
            first(h, d).wait_send()
            second(h, d).wait_send()


def shards(term_matrix, sign_bits, sampled):
    vmem = pl.BlockSpec(memory_space=pltpu.VMEM)
    dma = pltpu.SemaphoreType.DMA
    return pl.pallas_call(
        kernel,
        out_shape=jax.ShapeDtypeStruct((32, 2048), F32),
        in_specs=[pl.BlockSpec(memory_space=pl.ANY), vmem, vmem],
        out_specs=vmem,
        scratch_shapes=[
            pltpu.VMEM((768, 2048), BF16),
            pltpu.VMEM((2048, 512), BF16),
            pltpu.VMEM((2, 384, 256), F32),
            pltpu.VMEM((2, 384, 256), F32),
            pltpu.VMEM((2, 384, 256), F32),
            pltpu.VMEM((2, 8, 112, 128), jnp.int16),
            pltpu.VMEM((2, 8, 112, 128), jnp.int16),
            pltpu.VMEM((2, 16, 48, 256), BF16),
            pltpu.VMEM((512, 768), BF16),
            pltpu.VMEM((1280, 128), F32),
            pltpu.VMEM((16, 40, 128), F32),
            pltpu.VMEM((1280, 128), F32),
            pltpu.VMEM((16, 128, 128), F32),
            pltpu.VMEM((32, 8, 128), F32),
            pltpu.VMEM((64, 8, 128), F32),
            pltpu.VMEM((512, 2048), F32),
            pltpu.VMEM((2, 4, 4, 272, 128), jnp.int16),
            pltpu.VMEM((2, 4, 4, 272, 128), jnp.int16),
            pltpu.VMEM((2, 4, 272, 128), jnp.int16),
            pltpu.VMEM((2, 4, 272, 128), jnp.int16),
            pltpu.VMEM((2, 4, 256, 128), F32),
            pltpu.VMEM((512, 128), F32),
            pltpu.VMEM((16, 32, 128), F32),
            dma((2,)),
        ]
        + [dma((2,))] * 2
        + [dma((2, 8))] * 6
        + [dma((16,))] * 6
        + [dma((2, 4))] * 4
        + [dma((16,))] * 2,
        compiler_params=pltpu.CompilerParams(collective_id=0, has_side_effects=True, vmem_limit_bytes=48 << 20),
    )(term_matrix, sign_bits.reshape(1, 2048), sampled)


def solution(mesh):
    in_specs = (P("row", "col"), P("col"), P("col", None))
    return jax.shard_map(shards, mesh=mesh, in_specs=in_specs, out_specs=P("row", "col"), check_vma=False)
```

time: 492 us -> 88.2 us (0.18); the launches traced: 487 us -> 88 us
  waiting for transfers between devices: 295 us -> 0 us
  other arithmetic: 125 us -> 0 us
  Pallas kernels: 0 us -> 83.9 us
  matrix products: 29.3 us -> 0 us
  between operations: 16.3 us -> 0.01 us
  local copies, waits for them, and re-layouts: 18.2 us -> 4.05 us
    psum x2 -> x0, waiting for transfers between devices: 213 us -> none  [the longest x1 117 us: shards(): sketch = lax.psum(partial_sketch, 'col')]
    another operation x17 -> x0, other arithmetic: 119 us -> none  [the longest x14 78.6 us: shards(): basis_t = basis_from(jnp.linalg.cholesky(gram_sum), sketch)]
    pallas_call x0 -> x1, Pallas kernels: none -> 83.9 us  [shards(): pl.pallas_call(kernel, out_shape=jax.ShapeDtypeStruct((32, 2048), F32), i...]
    reduce_scatter x1 -> x0, waiting for transfers between devices: 81.9 us -> none  [shards(): lax.psum_scatter(jnp.dot(basis_t, term_matrix, preferred_element_type=jnp...]
    another operation x13 -> x0, matrix products: 14.7 us -> none  [the longest x7 9.29 us: basis_from(): jax.scipy.linalg.solve_triangular(factor, sketch_part.T, lower=True)]
    dot_general x4 -> x0, matrix products: 14.5 us -> none  [the longest x1 5.6 us: gram_of(): jnp.dot(sketch_part.T, sketch_part, precision=lax.Precision.HIGHEST, pref...]
    another operation x17 -> x0, local copies, waits for them, and re-layouts: 11.7 us -> none
  transfers between devices with their start and end apart: 3 -> 0, of which waited for: 3 -> 0; matrix products, arithmetic and copies ran while one was open for 0% -> 0% of each run, Pallas kernels for 0% -> 0%
where the time goes in v2:
time: 88.2 us; the launch traced here: 88 us
  Pallas kernels  83.9 us (95%)
  local copies, waits for them, and re-layouts  4.05 us (5%)
    pallas_call x1, Pallas kernels, shards(): pl.pallas_call(kernel, out_shape=jax.ShapeDtypeStruct((32, 2048), F32), i...  83.9 us
    unnamed x7, local copies, waits for them, and re-layouts  4.05 us

profile of v2, /device:TPU:1, one launch (start us, length us, event | category | flops | bytes accessed | tf_op | source)
XLA Modules:
  0.0 88.0 jit_solution(3528704615587807071)
XLA Ops:
  0.0 0.0 copy-start
  0.0 1.9 %copy-done = bf16[768,2048]{1,0:T(8,128)(2,1)S(1)} copy-done((bf16[768,2048]{1,0:T(8,128)(2,1)S(1)}, bf16[768,2048]{1,0:T(8,128)(2,1)}, u32[]{:S(2)}) %copy-start) | copy-done | bytes 3145752
  1.9 0.0 copy-start.1
  1.9 0.8 copy-done.1
  2.6 0.0 copy-start.2
  2.7 0.7 copy-done.2
  3.3 83.9 %shard_map.37 = f32[32,2048]{1,0:T(8,128)S(1)} custom-call(bf16[768,2048]{1,0:T(8,128)(2,1)S(1)} %copy-done, s32[1,2048]{1,0:T(1,128)S(1)} %bitcast.1, s32[16,512]{1,0:T(8,128)S(1)} %copy-done.1), custom_call_target="tpu_custom_call" | custom-call | tf_op jit(solution)/shard_map/pallas_call | solution.py:361
  87.3 0.7 copy.5
Async XLA Ops:
  0.0 1.9 %copy-start = (bf16[768,2048]{1,0:T(8,128)(2,1)S(1)}, bf16[768,2048]{1,0:T(8,128)(2,1)}, u32[]{:S(2)}) copy-start(bf16[768,2048]{1,0:T(8,128)(2,1)} %a_hbm.1) | copy-start | bytes 9437188
  1.9 0.8 copy-start.1
  2.6 0.7 copy-start.2

commit v3 on v2

--- a/solution.py
+++ b/solution.py
@@ -27,11 +27,19 @@
     return copy
 
 
-def pack(value):
+def power_of(value):
     top = jnp.max(jnp.max(jnp.abs(value), axis=0, keepdims=True), axis=1, keepdims=True)
-    power = jnp.ceil(jnp.log(jnp.maximum(top, 1e-30)) * (1.0 / LN2)) - 14.0
-    coded = jnp.floor(value * jnp.exp(power * -LN2) + 0.5).astype(jnp.int32).astype(jnp.int16)
-    return coded, jnp.broadcast_to(power, (16, 128)).astype(jnp.int32).astype(jnp.int16)
+    return jnp.ceil(jnp.log(jnp.maximum(top, 1e-30)) * (1.0 / LN2)) - 14.0
+
+
+def coded(value, power):
+    return jnp.floor(value * jnp.exp(power * -LN2) + 0.5).astype(jnp.int32).astype(jnp.int16)
+
+
+def pack(value, ref, at):
+    power = power_of(value)
+    ref[at + (slice(0, 256),)] = coded(value, power)
+    ref[at + (slice(256, 272),)] = jnp.broadcast_to(power, (16, 128)).astype(jnp.int32).astype(jnp.int16)
 
 
 def step_of(power):
@@ -145,14 +153,14 @@
 TRI = [(i, j) for i in range(4) for j in range(i, 4)]
 FAR_FIRST = (4, 3, 5, 2, 6, 1, 7)
 NEAR_FIRST = FAR_FIRST[::-1]
-MID = 2
+MID = 3
 
 
 def kernel(
-    a_hbm, sign_ref, samp_ref, o_ref,
-    a, om, mate_out, mate_in, own, part_out, part_in, full, yt, gloc, gin, gfull, gsq, x, w,
+    a_hbm, sign_hbm, samp_hbm, o_ref,
+    a, sign_ref, samp_ref, om, mate_out, mate_in, own, part_out, part_in, step_out, step_in, full, yt, gloc, gin, gfull, gsq, x, w,
     zf, zs1, zr1, zs2, zr2, zown, pbuf, obuf,
-    s_a, s_mate, r_mate, s_part, r_part, s_full, r_full, s_fwd, r_fwd,
+    s_a, s_mate, r_mate, s_part, r_part, s_step, r_step, s_full, r_full, s_fwd, r_fwd,
     s_c, r_c, s_d, r_d, s_e, r_e, s_z1, r_z1, s_z2, r_z2, s_o, r_o,
 ):
     row, col = lax.axis_index("row"), lax.axis_index("col")
@@ -169,12 +177,21 @@
     def half_rows(which):
         return pl.ds(pl.multiple_of(which * 384, 384), 384)
 
+    small = [
+        pltpu.make_async_copy(samp_hbm, samp_ref, s_a.at[2]),
+        pltpu.make_async_copy(sign_hbm, sign_ref, s_a.at[3]),
+    ]
+    for load in small:
+        load.start()
     loads = []
     for n, which in enumerate((1 - core, core)):
         loads.append(pltpu.make_async_copy(a_hbm.at[half_rows(which)], a.at[half_rows(which)], s_a.at[n]))
         loads[n].start()
     ready = barrier([mate] + [chip(d) for d in range(1, 8)] + [(peer(d), col) for d in range(1, 16)])
 
+    for load in small:
+        load.wait()
+
     term = lax.broadcasted_iota(jnp.int32, (128, 512), 0)
     for block in range(16):
         parity = lax.population_count(term & samp_ref[block : block + 1, :]) & 1
@@ -185,7 +202,7 @@
         rows = a[half_rows(which), :] * signs
         return jnp.dot(rows, om[:, 256 * n : 256 * n + 256], preferred_element_type=F32)
 
-    mate_copies, part_copies, full_copies, fwd_copies = [], [], [], []
+    mate_copies, part_copies, step_copies, full_copies, fwd_copies = [], [], [], [], []
     loads[0].wait()
     for n in range(2):
         mate_out[n] = partial(1 - core, n)
@@ -197,23 +214,23 @@
         own[n] = partial(core, n)
         mate_copies[n].wait_recv()
         own[n] += mate_in[n]
+        power = power_of(own[n])
+        step_out[n] = jnp.broadcast_to(jnp.exp(power * LN2), (1, 128))
         for d in FAR_FIRST:
             there = lax.rem(z + d, 8)
-            coded, power = pack(own[n, pl.ds(pl.multiple_of(there * 48, 48), 48), :])
-            part_out[n, d, 0:48, :] = coded[:, 0:128]
-            part_out[n, d, 48:96, :] = coded[:, 128:256]
-            part_out[n, d, 96:112, :] = power
+            part_out[n, d] = coded(own[n, pl.ds(pl.multiple_of(there * 48, 48), 48), :], power)
             part_copies.append(send(part_out.at[n, d], part_in.at[n, d], s_part.at[n, d], r_part.at[n, d], chip(d)))
+            step_copies.append(send(step_out.at[n], step_in.at[n, d], s_step.at[n, d], r_step.at[n, d], chip(d)))
     slot = core * 8 + z
     for n in range(2):
-        for copy in part_copies[7 * n : 7 * n + 7]:
+        for copy in part_copies[7 * n : 7 * n + 7] + step_copies[7 * n : 7 * n + 7]:
             copy.wait_recv()
         for j in range(2):
-            total = own[n, pl.ds(pl.multiple_of(z * 48, 48), 48), 128 * j : 128 * j + 128]
+            half = slice(128 * j, 128 * j + 128)
+            total = own[n, pl.ds(pl.multiple_of(z * 48, 48), 48), half]
             for d in range(1, 8):
-                value = part_in[n, d, 48 * j : 48 * j + 48, :].astype(jnp.int32).astype(F32)
-                total = total + value * step_of(part_in[n, d, 96:112, :])
-            full[n, slot, :, 128 * j : 128 * j + 128] = total.astype(BF16)
+                total = total + part_in[n, d, :, half].astype(jnp.int32).astype(F32) * step_in[n, d]
+            full[n, slot, :, half] = total.astype(BF16)
         mine = full.at[n, slot]
         for d in FAR_FIRST:
             full_copies.append(send(mine, mine, s_full.at[n, d], r_full.at[n, d], chip(d)))
@@ -271,9 +288,7 @@
 
         def code(m, carry):
             d, e = m // 4 + 1, lax.rem(m, 4)
-            coded, power = pack(z_part(h, along(h, d, e)))
-            zs1[h, d, e, 0:256, :] = coded
-            zs1[h, d, e, 256:272, :] = power
+            pack(z_part(h, along(h, d, e)), zs1, (h, d, e))
             return carry
 
         lax.fori_loop(0, 12, code, 0)
@@ -288,13 +303,13 @@
     for d in range(1, 16):
         d_copies.append(send(mine, mine, s_d.at[d], r_d.at[d], (peer(d), col)))
     e_copies.append(send(mine, mine, s_e.at[0], r_e.at[0], mate))
-    for d in (2, 1, 3):
-        for h in range(2):
-            first(h, d).start()
     for d in range(1, 16):
         d_copies[d - 1].wait_recv()
         came = gfull.at[piece(lax.rem(row + 16 - d, 16))]
         e_copies.append(send(came, came, s_e.at[d], r_e.at[d], mate))
+    for d in (2, 1, 3):
+        for h in range(2):
+            first(h, d).start()
     for copy in e_copies:
         copy.wait_recv()
     for n, (i, j) in enumerate(TRI):
@@ -314,9 +329,7 @@
                         step = step_of(zr1[h, f, e, 256:272, :])
                         value = value + zr1[h, f, e, 0:256, :].astype(jnp.int32).astype(F32) * step
                     zown[h, d] = value
-                    coded, power = pack(value)
-                    zs2[h, d, 0:256, :] = coded
-                    zs2[h, d, 256:272, :] = power
+                    pack(value, zs2, (h, d))
                     return carry
 
                 lax.fori_loop(0, 4, add, 0)
@@ -347,7 +360,7 @@
         copy.wait_recv()
     for r in range(16):
         o_ref[:, 128 * r : 128 * r + 128] = obuf[r]
-    for copy in mate_copies + part_copies + full_copies + fwd_copies + c_copies + d_copies + e_copies + o_copies:
+    for copy in mate_copies + part_copies + step_copies + full_copies + fwd_copies + c_copies + d_copies + e_copies + o_copies:
         copy.wait_send()
     for h in range(2):
         for d in range(1, 4):
@@ -361,16 +374,20 @@
     return pl.pallas_call(
         kernel,
         out_shape=jax.ShapeDtypeStruct((32, 2048), F32),
-        in_specs=[pl.BlockSpec(memory_space=pl.ANY), vmem, vmem],
+        in_specs=[pl.BlockSpec(memory_space=pl.ANY)] * 3,
         out_specs=vmem,
         scratch_shapes=[
             pltpu.VMEM((768, 2048), BF16),
+            pltpu.VMEM((1, 2048), jnp.int32),
+            pltpu.VMEM((16, 512), jnp.int32),
             pltpu.VMEM((2048, 512), BF16),
             pltpu.VMEM((2, 384, 256), F32),
             pltpu.VMEM((2, 384, 256), F32),
             pltpu.VMEM((2, 384, 256), F32),
-            pltpu.VMEM((2, 8, 112, 128), jnp.int16),
-            pltpu.VMEM((2, 8, 112, 128), jnp.int16),
+            pltpu.VMEM((2, 8, 48, 256), jnp.int16),
+            pltpu.VMEM((2, 8, 48, 256), jnp.int16),
+            pltpu.VMEM((2, 1, 128), F32),
+            pltpu.VMEM((2, 8, 1, 128), F32),
             pltpu.VMEM((2, 16, 48, 256), BF16),
             pltpu.VMEM((512, 768), BF16),
             pltpu.VMEM((1280, 128), F32),
@@ -387,14 +404,14 @@
             pltpu.VMEM((2, 4, 256, 128), F32),
             pltpu.VMEM((512, 128), F32),
             pltpu.VMEM((16, 32, 128), F32),
-            dma((2,)),
+            dma((4,)),
         ]
         + [dma((2,))] * 2
-        + [dma((2, 8))] * 6
+        + [dma((2, 8))] * 8
         + [dma((16,))] * 6
         + [dma((2, 4))] * 4
         + [dma((16,))] * 2,
-        compiler_params=pltpu.CompilerParams(collective_id=0, has_side_effects=True, vmem_limit_bytes=48 << 20),
+        compiler_params=pltpu.CompilerParams(collective_id=0, has_side_effects=True, vmem_limit_bytes=60 << 20),
     )(term_matrix, sign_bits.reshape(1, 2048), sampled)
 
 

time: 88.2 us -> 80.9 us (0.917)
  Pallas kernels: 83.9 us -> 79.1 us
  local copies, waits for them, and re-layouts: 4.05 us -> 1.67 us
    pallas_call x1, Pallas kernels: 83.9 us -> 79.1 us  [shards(): pl.pallas_call(kernel, out_shape=jax.ShapeDtypeStruct((32, 2048), F32), i...]
    unnamed x7 -> x1, local copies, waits for them, and re-layouts: 4.05 us -> 1.67 us
where the time goes in v3:
time: 80.9 us; the launch traced here: 80.8 us
  Pallas kernels  79.1 us (98%)
  local copies, waits for them, and re-layouts  1.67 us (2%)
    pallas_call x1, Pallas kernels, shards(): pl.pallas_call(kernel, out_shape=jax.ShapeDtypeStruct((32, 2048), F32), i...  79.1 us
    unnamed x1, local copies, waits for them, and re-layouts  1.67 us

profile of v3, /device:TPU:1, one launch (start us, length us, event | category | flops | bytes accessed | tf_op | source)
XLA Modules:
  0.0 80.8 jit_solution(14407507237610733835)
XLA Ops:
  0.0 79.1 %shard_map.37 = f32[32,2048]{1,0:T(8,128)} custom-call(bf16[768,2048]{1,0:T(8,128)(2,1)} %a_hbm.1, s32[1,2048]{1,0:T(1,128)} %bitcast.1, s32[16,512]{1,0:T(8,128)} %samp_hbm.1), custom_call_target="tpu_custom_call" | custom-call | tf_op jit(solution)/shard_map/pallas_call | solution.py:374
  79.1 1.7 %copy.5 = f32[32,2048]{1,0:T(8,128)} copy(f32[32,2048]{1,0:T(8,128)} %shard_map.37) | data formatting | bytes 524288

commit v4 on v3

--- a/solution.py
+++ b/solution.py
@@ -46,6 +46,9 @@
     return jnp.exp(power.astype(jnp.int32).astype(F32) * LN2)[0:1, :]
 
 
+AHEAD = 2
+
+
 def lane_of(x, lane):
     return jnp.broadcast_to(x[:, lane : lane + 1], (8, 128))
 
@@ -71,6 +74,14 @@
     left = jnp.concatenate([ah, ah, am, ah, am, al], 1)
     right = jnp.concatenate([bh, bm, bh, bl, bm, bh], 0)
     return jnp.dot(left, right, preferred_element_type=F32)
+
+
+def dot_mid(a, b, axis):
+    ah, am, _ = split(a)
+    bh, bm, _ = split(b)
+    left = jnp.concatenate([ah, ah, am], axis)
+    right = jnp.concatenate([bh, bm, bh], 0)
+    return lax.dot_general(left, right, (((axis,), (0,)), ((), ())), preferred_element_type=F32)
 
 
 def factor_block(x, w, base):
@@ -97,54 +108,47 @@
             for j in range(k + 1, 8):
                 rows[j] = rows[j] - mult[k][j] * rows[k]
         last = STRIPS * (t // STRIPS) + STRIPS
+        reach = min(last + AHEAD, 16)
         done = lanes < at + 8
         for k in range(8):
             u = rows[k] * lax.rsqrt(a[k][k])
             w[base // 8 + t, k : k + 1, :] = jnp.where(done, u, 0.0)[0:1]
-            if last < 16:
+            if reach < 16:
                 x[16 + t % STRIPS, k : k + 1, :] = jnp.where(done | (lanes >= 8 * last), u, 0.0)[0:1]
-        if t + 1 < last:
-            v = [None] * 8
-            for i in range(7, -1, -1):
-                v[i] = rows[i] * recips[i]
-                for j in range(7, i, -1):
-                    v[i] = v[i] - mult[i][j] * v[j]
-            for s in range(t + 1, last):
-                old = x[s]
-                new = jnp.where(here, 0.0, old)
-                for k in range(8):
-                    new = new - lane_of(old, at + k) * v[k]
-                x[s] = new
-        elif last < 16:
+        scaled = [rows[k] * recips[k] for k in range(8)]
+        for s in range(t + 1, reach):
+            old = x[s]
+            new = jnp.where(here, 0.0, old)
+            c = [lane_of(old, at + k) for k in range(8)]
+            for k in range(8):
+                for j in range(k):
+                    c[k] = c[k] - c[j] * mult[j][k]
+                new = new - c[k] * scaled[k]
+            x[s] = new
+        if t + 1 == last and reach < 16:
             u = x[16 : 16 + STRIPS].reshape(8 * STRIPS, 128)
-            change = dot_t(u, u)[8 * last :].reshape(16 - last, 8, 128)
+            change = dot_t(u, u)[8 * reach :].reshape(16 - reach, 8, 128)
             inside = (lanes >= 8 * (last - STRIPS)) & (lanes < 8 * last)
-            x[last:16] = jnp.where(inside[None], 0.0, x[last:16]) - change
+            x[reach:16] = jnp.where(inside[None], 0.0, x[reach:16]) - change
 
 
 def factor(g, x, w, between):
     def step(k, carry):
         between(k)
-        x[0:16] = g[5 * k].reshape(16, 8, 128)
+        x[0:16] = g[k, :, pl.ds(pl.multiple_of(128 * k, 128), 128)].reshape(16, 8, 128)
         factor_block(x, w, 128 * k)
-        inverse = w[pl.ds(16 * k, 16)].reshape(128, 128)
-
-        def panel(j, c):
-            g[4 * k + j] = dot_hi(inverse, g[4 * k + j])
-            return c
-
-        lax.fori_loop(k + 1, 4, panel, 0)
-
-        def outer(i, c):
-            left = g[4 * k + i]
-
-            def inner(j, cc):
-                g[4 * i + j] = g[4 * i + j] - dot_t(left, g[4 * k + j])
-                return cc
-
-            return lax.fori_loop(i, 4, inner, c)
-
-        lax.fori_loop(k + 1, 4, outer, 0)
+
+        @pl.when(k < 3)
+        def _():
+            panel = dot_hi(w[pl.ds(16 * k, 16)].reshape(128, 128), g[k])
+            g[k] = panel
+            change = dot_t(panel, panel)
+            for i in range(1, 4):
+
+                @pl.when(i > k)
+                def _():
+                    g[i] = g[i] - change[128 * i : 128 * i + 128]
+
         return carry
 
     lax.fori_loop(0, 4, step, 0)
@@ -159,9 +163,9 @@
 def kernel(
     a_hbm, sign_hbm, samp_hbm, o_ref,
     a, sign_ref, samp_ref, om, mate_out, mate_in, own, part_out, part_in, step_out, step_in, full, yt, gloc, gin, gfull, gsq, x, w,
-    zf, zs1, zr1, zs2, zr2, zown, pbuf, obuf,
+    zf, zs1, zr1, zt1, zu1, zs2, zr2, zown, pbuf, obuf,
     s_a, s_mate, r_mate, s_part, r_part, s_step, r_step, s_full, r_full, s_fwd, r_fwd,
-    s_c, r_c, s_d, r_d, s_e, r_e, s_z1, r_z1, s_z2, r_z2, s_o, r_o,
+    s_c, r_c, s_d, r_d, s_e, r_e, s_z1, r_z1, s_t1, r_t1, s_z2, r_z2, s_o, r_o,
 ):
     row, col = lax.axis_index("row"), lax.axis_index("col")
     z, core = col // 2, lax.rem(col, 2)
@@ -235,36 +239,41 @@
         for d in FAR_FIRST:
             full_copies.append(send(mine, mine, s_full.at[n, d], r_full.at[n, d], chip(d)))
         fwd_copies.append(send(mine, mine, s_fwd.at[n, 0], r_fwd.at[n, 0], mate))
+    def piece(r):
+        return pl.ds(pl.multiple_of(40 * (2 * r + core), 8), 40)
+
+    def gram(i, n):
+        blocks = jnp.dot(yt[128 * i : 128 * i + 128, :], full[n].reshape(768, 256), preferred_element_type=F32)
+        for j in range(2 * n, 2 * n + 2):
+            if j >= i:
+                at = 128 * TRI.index((i, j))
+                gloc[at : at + 128, :] = blocks[:, 128 * (j - 2 * n) : 128 * (j - 2 * n) + 128]
+
+    def product(h):
+        def columns(m, carry):
+            cols = pl.ds(pl.multiple_of(256 * m, 256), 256)
+            zf[256 * h : 256 * h + 256, cols] = jnp.dot(yt[256 * h : 256 * h + 256, :], a[:, cols], preferred_element_type=F32)
+            return carry
+
+        lax.fori_loop(0, 8, columns, 0)
+
+    c_copies, d_copies, e_copies = [], [], []
     for n in range(2):
         for m, d in enumerate(FAR_FIRST):
             full_copies[7 * n + m].wait_recv()
             came = full.at[n, core * 8 + lax.rem(z + 8 - d, 8)]
             fwd_copies.append(send(came, came, s_fwd.at[n, d], r_fwd.at[n, d], mate))
-    for copy in fwd_copies:
-        copy.wait_recv()
-
-    def piece(r):
-        return pl.ds(pl.multiple_of(40 * (2 * r + core), 8), 40)
-
-    for i in range(4):
-        yt[128 * i : 128 * i + 128, :] = full[i // 2, :, :, 128 * (i % 2) : 128 * (i % 2) + 128].reshape(768, 128).T
-    for i in range(4):
-        for n in range(i // 2, 2):
-            blocks = jnp.dot(yt[128 * i : 128 * i + 128, :], full[n].reshape(768, 256), preferred_element_type=F32)
-            for j in range(2 * n, 2 * n + 2):
-                if j >= i:
-                    at = 128 * TRI.index((i, j))
-                    gloc[at : at + 128, :] = blocks[:, 128 * (j - 2 * n) : 128 * (j - 2 * n) + 128]
-    c_copies, d_copies, e_copies, o_copies = [], [], [], []
+        for copy in fwd_copies[n : n + 1] + fwd_copies[2 + 7 * n : 9 + 7 * n]:
+            copy.wait_recv()
+        for i in range(2 * n, 2 * n + 2):
+            yt[128 * i : 128 * i + 128, :] = full[n, :, :, 128 * (i % 2) : 128 * (i % 2) + 128].reshape(768, 128).T
+        for i in range(2 * n + 2):
+            gram(i, n)
+        if n == 0:
+            product(0)
     for d in range(1, 16):
         c_copies.append(send(gloc.at[piece(peer(d))], gin.at[d], s_c.at[d], r_c.at[d], (peer(d), col)))
-
-    def product(n, carry):
-        cols = pl.ds(pl.multiple_of(256 * n, 256), 256)
-        zf[:, cols] = jnp.dot(yt[...], a[:, cols], preferred_element_type=F32)
-        return carry
-
-    lax.fori_loop(0, 8, product, 0)
+    product(1)
 
     def along(h, d, e):
         return (4 * e + lax.rem(px + d, 4)) if h == 0 else (4 * lax.rem(py + d, 4) + e)
@@ -275,6 +284,12 @@
             src_ref=zs1.at[h, d], dst_ref=zr1.at[h, d], send_sem=s_z1.at[h, d], recv_sem=r_z1.at[h, d], device_id=target, device_id_type=MESH
         )
 
+    def first_steps(h, d):
+        target = (along(h, d, py if h == 0 else px), col)
+        return pltpu.make_async_remote_copy(
+            src_ref=zt1.at[h, d], dst_ref=zu1.at[h, d], send_sem=s_t1.at[h, d], recv_sem=r_t1.at[h, d], device_id=target, device_id_type=MESH
+        )
+
     def second(h, d):
         target = (along(1 - h, d, px if h == 0 else py), col)
         return pltpu.make_async_remote_copy(
@@ -288,7 +303,10 @@
 
         def code(m, carry):
             d, e = m // 4 + 1, lax.rem(m, 4)
-            pack(z_part(h, along(h, d, e)), zs1, (h, d, e))
+            value = z_part(h, along(h, d, e))
+            power = power_of(value)
+            zs1[h, d, e] = coded(value, power)
+            zt1[h, d, e] = jnp.broadcast_to(jnp.exp(power * LN2), (1, 128))
             return carry
 
         lax.fori_loop(0, 12, code, 0)
@@ -309,11 +327,14 @@
         e_copies.append(send(came, came, s_e.at[d], r_e.at[d], mate))
     for d in (2, 1, 3):
         for h in range(2):
+            first_steps(h, d).start()
             first(h, d).start()
     for copy in e_copies:
         copy.wait_recv()
+    for i in range(1, 4):
+        gsq[i, :, 0 : 128 * i] = jnp.zeros((128, 128 * i), F32)
     for n, (i, j) in enumerate(TRI):
-        gsq[4 * i + j] = gfull[128 * n : 128 * n + 128, :]
+        gsq[i, :, 128 * j : 128 * j + 128] = gfull[128 * n : 128 * n + 128, :]
 
     def between(k):
         @pl.when(k == MID)
@@ -321,13 +342,13 @@
             for h in range(2):
                 for d in range(1, 4):
                     first(h, d).wait_recv()
+                    first_steps(h, d).wait_recv()
 
                 def add(d, carry):
                     e = lax.rem((py if h == 0 else px) + d, 4)
                     value = z_part(h, along(h, 0, e))
                     for f in range(1, 4):
-                        step = step_of(zr1[h, f, e, 256:272, :])
-                        value = value + zr1[h, f, e, 0:256, :].astype(jnp.int32).astype(F32) * step
+                        value = value + zr1[h, f, e].astype(jnp.int32).astype(F32) * zu1[h, f, e]
                     zown[h, d] = value
                     pack(value, zs2, (h, d))
                     return carry
@@ -338,33 +359,54 @@
 
     factor(gsq, x, w, between)
 
-    for h in range(2):
-        for d in range(1, 4):
-            second(h, d).wait_recv()
-        value = zown[h, 0]
-        for d in range(1, 4):
-            step = step_of(zr2[h, d, 256:272, :])
-            value = value + zr2[h, d, 0:256, :].astype(jnp.int32).astype(F32) * step
-        pbuf[256 * h : 256 * h + 256, :] = value
+    def out_copy(there, here):
+        return pltpu.make_async_remote_copy(
+            src_ref=pbuf.at[pl.ds(pl.multiple_of(32 * there, 32), 32)], dst_ref=obuf.at[here],
+            send_sem=s_o.at[there], recv_sem=r_o.at[here], device_id=(there, col), device_id_type=MESH,
+        )
+
     for k in range(4):
-        solved = dot_hi(w[16 * k : 16 * k + 16].reshape(128, 128), pbuf[128 * k : 128 * k + 128, :])
+        h = k // 2
+        if k % 2 == 0:
+            for d in range(1, 4):
+                second(h, d).wait_recv()
+            value = zown[h, 0]
+            for d in range(1, 4):
+                step = step_of(zr2[h, d, 256:272, :])
+                value = value + zr2[h, d, 0:256, :].astype(jnp.int32).astype(F32) * step
+            if h == 1:
+                for j in range(2):
+                    value = value - dot_mid(gsq[j, :, 256:512], pbuf[128 * j : 128 * j + 128, :], 0)
+            pbuf[256 * h : 256 * h + 256, :] = value
+        solved = dot_mid(w[16 * k : 16 * k + 16].reshape(128, 128), pbuf[128 * k : 128 * k + 128, :], 1)
         pbuf[128 * k : 128 * k + 128, :] = solved
-        for j in range(k + 1, 4):
-            pbuf[128 * j : 128 * j + 128, :] -= dot_t(gsq[4 * k + j], solved)
-
+        for there in range(4 * k, 4 * k + 4):
+
+            @pl.when(row != there)
+            def _():
+                out_copy(there, row).start()
+
+        if k % 2 == 0:
+            after = slice(128 * k + 128, 128 * k + 256)
+            pbuf[after, :] -= dot_mid(gsq[k, :, after], solved, 0)
+
+    obuf[row] = pbuf[pl.ds(pl.multiple_of(32 * row, 32), 32), :]
     for d in range(1, 16):
-        part = pl.ds(pl.multiple_of(32 * peer(d), 32), 32)
-        o_copies.append(send(pbuf.at[part], obuf.at[row], s_o.at[d], r_o.at[d], (peer(d), col)))
-    obuf[row] = pbuf[pl.ds(pl.multiple_of(32 * row, 32), 32), :]
-    for copy in o_copies:
-        copy.wait_recv()
+        out_copy(row, peer(d)).wait_recv()
     for r in range(16):
         o_ref[:, 128 * r : 128 * r + 128] = obuf[r]
-    for copy in mate_copies + part_copies + step_copies + full_copies + fwd_copies + c_copies + d_copies + e_copies + o_copies:
+    for copy in mate_copies + part_copies + step_copies + full_copies + fwd_copies + c_copies + d_copies + e_copies:
         copy.wait_send()
+    for there in range(16):
+
+        @pl.when(row != there)
+        def _():
+            out_copy(there, row).wait_send()
+
     for h in range(2):
         for d in range(1, 4):
             first(h, d).wait_send()
+            first_steps(h, d).wait_send()
             second(h, d).wait_send()
 
 
@@ -393,12 +435,14 @@
             pltpu.VMEM((1280, 128), F32),
             pltpu.VMEM((16, 40, 128), F32),
             pltpu.VMEM((1280, 128), F32),
-            pltpu.VMEM((16, 128, 128), F32),
+            pltpu.VMEM((4, 128, 512), F32),
             pltpu.VMEM((32, 8, 128), F32),
             pltpu.VMEM((64, 8, 128), F32),
             pltpu.VMEM((512, 2048), F32),
-            pltpu.VMEM((2, 4, 4, 272, 128), jnp.int16),
-            pltpu.VMEM((2, 4, 4, 272, 128), jnp.int16),
+            pltpu.VMEM((2, 4, 4, 256, 128), jnp.int16),
+            pltpu.VMEM((2, 4, 4, 256, 128), jnp.int16),
+            pltpu.VMEM((2, 4, 4, 1, 128), F32),
+            pltpu.VMEM((2, 4, 4, 1, 128), F32),
             pltpu.VMEM((2, 4, 272, 128), jnp.int16),
             pltpu.VMEM((2, 4, 272, 128), jnp.int16),
             pltpu.VMEM((2, 4, 256, 128), F32),
@@ -409,7 +453,7 @@
         + [dma((2,))] * 2
         + [dma((2, 8))] * 8
         + [dma((16,))] * 6
-        + [dma((2, 4))] * 4
+        + [dma((2, 4))] * 6
         + [dma((16,))] * 2,
         compiler_params=pltpu.CompilerParams(collective_id=0, has_side_effects=True, vmem_limit_bytes=60 << 20),
     )(term_matrix, sign_bits.reshape(1, 2048), sampled)

time: 80.9 us -> 77 us (0.952)
  Pallas kernels: 79.1 us -> 75 us
    pallas_call x1, Pallas kernels: 79.1 us -> 75 us  [shards(): pl.pallas_call(kernel, out_shape=jax.ShapeDtypeStruct((32, 2048), F32), i...]
where the time goes in v4:
time: 77 us; the launch traced here: 76.7 us
  Pallas kernels  75 us (97%)
  local copies, waits for them, and re-layouts  1.67 us (2%)
    pallas_call x1, Pallas kernels, shards(): pl.pallas_call(kernel, out_shape=jax.ShapeDtypeStruct((32, 2048), F32), i...  75 us
    unnamed x1, local copies, waits for them, and re-layouts  1.67 us

profile of v4, /device:TPU:1, one launch (start us, length us, event | category | flops | bytes accessed | tf_op | source)
XLA Modules:
  0.0 76.7 jit_solution(16888939940719123373)
XLA Ops:
  0.0 75.0 %shard_map.37 = f32[32,2048]{1,0:T(8,128)} custom-call(bf16[768,2048]{1,0:T(8,128)(2,1)} %a_hbm.1, s32[1,2048]{1,0:T(1,128)} %bitcast.1, s32[16,512]{1,0:T(8,128)} %samp_hbm.1), custom_call_target="tpu_custom_call" | custom-call | tf_op jit(solution)/shard_map/pallas_call | solution.py:416
  75.1 1.7 %copy.5 = f32[32,2048]{1,0:T(8,128)} copy(f32[32,2048]{1,0:T(8,128)} %shard_map.37) | data formatting | bytes 524288

commit v5 on v4

--- a/solution.py
+++ b/solution.py
@@ -55,33 +55,23 @@
 
 def split(u):
     high = u.astype(BF16)
-    rest = u - high.astype(F32)
-    mid = rest.astype(BF16)
-    return high, mid, (rest - mid.astype(F32)).astype(BF16)
+    return high, (u - high.astype(F32)).astype(BF16)
 
 
 def dot_t(a, b):
-    ah, am, al = split(a)
-    bh, bm, bl = split(b)
-    left = jnp.concatenate([ah, ah, am, ah, am, al], 0)
-    right = jnp.concatenate([bh, bm, bh, bl, bm, bh], 0)
+    ah, am = split(a)
+    bh, bm = split(b)
+    left = jnp.concatenate([ah, ah, am], 0)
+    right = jnp.concatenate([bh, bm, bh], 0)
     return lax.dot_general(left, right, (((0,), (0,)), ((), ())), preferred_element_type=F32)
 
 
 def dot_hi(a, b):
-    ah, am, al = split(a)
-    bh, bm, bl = split(b)
-    left = jnp.concatenate([ah, ah, am, ah, am, al], 1)
-    right = jnp.concatenate([bh, bm, bh, bl, bm, bh], 0)
+    ah, am = split(a)
+    bh, bm = split(b)
+    left = jnp.concatenate([ah, ah, am], 1)
+    right = jnp.concatenate([bh, bm, bh], 0)
     return jnp.dot(left, right, preferred_element_type=F32)
-
-
-def dot_mid(a, b, axis):
-    ah, am, _ = split(a)
-    bh, bm, _ = split(b)
-    left = jnp.concatenate([ah, ah, am], axis)
-    right = jnp.concatenate([bh, bm, bh], 0)
-    return lax.dot_general(left, right, (((axis,), (0,)), ((), ())), preferred_element_type=F32)
 
 
 def factor_block(x, w, base):
@@ -263,14 +253,14 @@
             full_copies[7 * n + m].wait_recv()
             came = full.at[n, core * 8 + lax.rem(z + 8 - d, 8)]
             fwd_copies.append(send(came, came, s_fwd.at[n, d], r_fwd.at[n, d], mate))
+        if n == 1:
+            product(0)
         for copy in fwd_copies[n : n + 1] + fwd_copies[2 + 7 * n : 9 + 7 * n]:
             copy.wait_recv()
         for i in range(2 * n, 2 * n + 2):
             yt[128 * i : 128 * i + 128, :] = full[n, :, :, 128 * (i % 2) : 128 * (i % 2) + 128].reshape(768, 128).T
         for i in range(2 * n + 2):
             gram(i, n)
-        if n == 0:
-            product(0)
     for d in range(1, 16):
         c_copies.append(send(gloc.at[piece(peer(d))], gin.at[d], s_c.at[d], r_c.at[d], (peer(d), col)))
     product(1)
@@ -344,18 +334,16 @@
                     first(h, d).wait_recv()
                     first_steps(h, d).wait_recv()
 
-                def add(d, carry):
+                for d in (2, 1, 3, 0):
                     e = lax.rem((py if h == 0 else px) + d, 4)
                     value = z_part(h, along(h, 0, e))
                     for f in range(1, 4):
                         value = value + zr1[h, f, e].astype(jnp.int32).astype(F32) * zu1[h, f, e]
-                    zown[h, d] = value
-                    pack(value, zs2, (h, d))
-                    return carry
-
-                lax.fori_loop(0, 4, add, 0)
-                for d in range(1, 4):
-                    second(h, d).start()
+                    if d == 0:
+                        zown[h] = value
+                    else:
+                        pack(value, zs2, (h, d))
+                        second(h, d).start()
 
     factor(gsq, x, w, between)
 
@@ -370,15 +358,15 @@
         if k % 2 == 0:
             for d in range(1, 4):
                 second(h, d).wait_recv()
-            value = zown[h, 0]
+            value = zown[h]
             for d in range(1, 4):
                 step = step_of(zr2[h, d, 256:272, :])
                 value = value + zr2[h, d, 0:256, :].astype(jnp.int32).astype(F32) * step
             if h == 1:
                 for j in range(2):
-                    value = value - dot_mid(gsq[j, :, 256:512], pbuf[128 * j : 128 * j + 128, :], 0)
+                    value = value - dot_t(gsq[j, :, 256:512], pbuf[128 * j : 128 * j + 128, :])
             pbuf[256 * h : 256 * h + 256, :] = value
-        solved = dot_mid(w[16 * k : 16 * k + 16].reshape(128, 128), pbuf[128 * k : 128 * k + 128, :], 1)
+        solved = dot_hi(w[16 * k : 16 * k + 16].reshape(128, 128), pbuf[128 * k : 128 * k + 128, :])
         pbuf[128 * k : 128 * k + 128, :] = solved
         for there in range(4 * k, 4 * k + 4):
 
@@ -388,7 +376,7 @@
 
         if k % 2 == 0:
             after = slice(128 * k + 128, 128 * k + 256)
-            pbuf[after, :] -= dot_mid(gsq[k, :, after], solved, 0)
+            pbuf[after, :] -= dot_t(gsq[k, :, after], solved)
 
     obuf[row] = pbuf[pl.ds(pl.multiple_of(32 * row, 32), 32), :]
     for d in range(1, 16):
@@ -445,7 +433,7 @@
             pltpu.VMEM((2, 4, 4, 1, 128), F32),
             pltpu.VMEM((2, 4, 272, 128), jnp.int16),
             pltpu.VMEM((2, 4, 272, 128), jnp.int16),
-            pltpu.VMEM((2, 4, 256, 128), F32),
+            pltpu.VMEM((2, 256, 128), F32),
             pltpu.VMEM((512, 128), F32),
             pltpu.VMEM((16, 32, 128), F32),
             dma((4,)),

time: 77 us -> 75.5 us (0.981)
  Pallas kernels: 75 us -> 73.5 us
    pallas_call x1, Pallas kernels: 75 us -> 73.5 us  [shards(): pl.pallas_call(kernel, out_shape=jax.ShapeDtypeStruct((32, 2048), F32), i...]
where the time goes in v5:
time: 75.5 us; the launch traced here: 75.2 us
  Pallas kernels  73.5 us (97%)
  local copies, waits for them, and re-layouts  1.67 us (2%)
    pallas_call x1, Pallas kernels, shards(): pl.pallas_call(kernel, out_shape=jax.ShapeDtypeStruct((32, 2048), F32), i...  73.5 us
    unnamed x1, local copies, waits for them, and re-layouts  1.67 us

profile of v5, /device:TPU:1, one launch (start us, length us, event | category | flops | bytes accessed | tf_op | source)
XLA Modules:
  0.0 75.2 jit_solution(2731568187985130998)
XLA Ops:
  0.0 73.5 %shard_map.37 = f32[32,2048]{1,0:T(8,128)} custom-call(bf16[768,2048]{1,0:T(8,128)(2,1)} %a_hbm.1, s32[1,2048]{1,0:T(1,128)} %bitcast.1, s32[16,512]{1,0:T(8,128)} %samp_hbm.1), custom_call_target="tpu_custom_call" | custom-call | tf_op jit(solution)/shard_map/pallas_call | solution.py:404
  73.5 1.7 %copy.5 = f32[32,2048]{1,0:T(8,128)} copy(f32[32,2048]{1,0:T(8,128)} %shard_map.37) | data formatting | bytes 524288

commit v6 on v5

--- a/solution.py
+++ b/solution.py
@@ -301,6 +301,10 @@
 
         lax.fori_loop(0, 12, code, 0)
 
+    for copy in mate_copies + part_copies + step_copies + full_copies + fwd_copies:
+        copy.wait_send()
+    for i in range(1, 4):
+        gsq[i, :, 0 : 128 * i] = jnp.zeros((128, 128 * i), F32)
     for copy in c_copies:
         copy.wait_recv()
     total = gloc[piece(row), :]
@@ -311,6 +315,8 @@
     for d in range(1, 16):
         d_copies.append(send(mine, mine, s_d.at[d], r_d.at[d], (peer(d), col)))
     e_copies.append(send(mine, mine, s_e.at[0], r_e.at[0], mate))
+    for copy in c_copies:
+        copy.wait_send()
     for d in range(1, 16):
         d_copies[d - 1].wait_recv()
         came = gfull.at[piece(lax.rem(row + 16 - d, 16))]
@@ -321,8 +327,6 @@
             first(h, d).start()
     for copy in e_copies:
         copy.wait_recv()
-    for i in range(1, 4):
-        gsq[i, :, 0 : 128 * i] = jnp.zeros((128, 128 * i), F32)
     for n, (i, j) in enumerate(TRI):
         gsq[i, :, 128 * j : 128 * j + 128] = gfull[128 * n : 128 * n + 128, :]
 
@@ -346,6 +350,12 @@
                         second(h, d).start()
 
     factor(gsq, x, w, between)
+    for copy in d_copies + e_copies:
+        copy.wait_send()
+    for h in range(2):
+        for d in range(1, 4):
+            first(h, d).wait_send()
+            first_steps(h, d).wait_send()
 
     def out_copy(there, here):
         return pltpu.make_async_remote_copy(
@@ -383,8 +393,6 @@
         out_copy(row, peer(d)).wait_recv()
     for r in range(16):
         o_ref[:, 128 * r : 128 * r + 128] = obuf[r]
-    for copy in mate_copies + part_copies + step_copies + full_copies + fwd_copies + c_copies + d_copies + e_copies:
-        copy.wait_send()
     for there in range(16):
 
         @pl.when(row != there)
@@ -393,8 +401,6 @@
 
     for h in range(2):
         for d in range(1, 4):
-            first(h, d).wait_send()
-            first_steps(h, d).wait_send()
             second(h, d).wait_send()
 
 

time: 75.5 us -> 75.4 us (level)
  no operation moved by 1% of the time
where the time goes in v6:
time: 75.4 us; the launch traced here: 75.2 us
  Pallas kernels  73.5 us (97%)
  local copies, waits for them, and re-layouts  1.67 us (2%)
    pallas_call x1, Pallas kernels, shards(): pl.pallas_call(kernel, out_shape=jax.ShapeDtypeStruct((32, 2048), F32), i...  73.5 us
    unnamed x1, local copies, waits for them, and re-layouts  1.67 us

profile of v6, /device:TPU:1, one launch (start us, length us, event | category | flops | bytes accessed | tf_op | source)
XLA Modules:
  0.0 75.2 jit_solution(15448887534088148637)
XLA Ops:
  0.0 73.5 %shard_map.37 = f32[32,2048]{1,0:T(8,128)} custom-call(bf16[768,2048]{1,0:T(8,128)(2,1)} %a_hbm.1, s32[1,2048]{1,0:T(1,128)} %bitcast.1, s32[16,512]{1,0:T(8,128)} %samp_hbm.1), custom_call_target="tpu_custom_call" | custom-call | tf_op jit(solution)/shard_map/pallas_call | solution.py:410
  73.5 1.7 %copy.5 = f32[32,2048]{1,0:T(8,128)} copy(f32[32,2048]{1,0:T(8,128)} %shard_map.37) | data formatting | bytes 524288
